TPU v7x, 32 devices: a whole 2x2x4 slice. The times are simulated.
32 devices in a mesh: logger: 4 (over y, x), seq: 2 (over core), vocab: 4 (over z).
Axes of the slice: x: 2, y: 2, z: 4, core: 2. Of those that a mesh axis runs over, the one named last changes fastest.
Arguments:
- hidden: bfloat16 [4, 64, 4096], P('logger', ('seq', 'vocab'))
- head_weight: bfloat16 [4, 4096, 4096], P('logger', None, ('seq', 'vocab')), may hold values from -0.09375 to 0.09375
- logged_tokens: int32 [64], replicated, may hold values from 0 to 4095
- logger_share: float32 [4], replicated, may hold values from 0.1 to 1
Outputs:
- log_weight: float32 [4, 64], P('logger', ('seq', 'vocab'))
All inputs are finite; a program needn't handle non-finite values.
Results may differ from a plain program's by a relative error of at most 0.00045.
Values may be sent and summed in bfloat16 or wider, within the bound.
A program may use at most 64 MiB of HBM per device.

v0:
```python
import jax
import jax.numpy as jnp
from jax import lax
from jax.sharding import PartitionSpec as P


def prefix(part, axis, combine, identity):
    place = lax.axis_index(axis)
    gathered = lax.all_gather(part, axis)
    state = jnp.zeros_like(part) + jnp.asarray(identity, part.dtype)

    def one(hop, state):
        return combine(state, lax.dynamic_index_in_dim(gathered, hop, 0, False))

    return lax.fori_loop(0, place, one, state)


def place(buffer, values, start):
    return values


def add_values(earlier, later):
    return earlier + later


def on_device(hidden, head_weight, logged_tokens, logger_share):
    token_rows = hidden[0]
    weight = head_weight[0]
    col_count = weight.shape[1]
    per_device = token_rows.shape[0]
    total_tokens = logged_tokens.shape[0]
    position = lax.axis_index(("seq", "vocab"))
    column_ids = position * col_count + lax.broadcasted_iota(jnp.int32, (1, col_count), 1)
    zeros = jnp.zeros((total_tokens,), jnp.float32)
    start_carry = (zeros, zeros, zeros)
    start = jnp.int32(0)
    logits = jnp.dot(
        lax.all_gather(token_rows, ("seq", "vocab"), axis=0, tiled=True),
        weight,
        preferred_element_type=jnp.float32,
    )
    block_max = jnp.max(logits, axis=1)
    block_sum = jnp.sum(jnp.exp(logits - block_max[:, None]), axis=1)
    block_pick = jnp.sum(jnp.where(logged_tokens[:, None] == column_ids, logits, 0.0), axis=1)
    stats = (
        place(start_carry[0], block_max, start),
        place(start_carry[1], block_sum, start),
        place(start_carry[2], block_pick, start),
    )
    local_max, local_sum, local_pick = stats
    offset = position * per_device
    whole_max = lax.pmax(local_max, ("seq", "vocab"))
    scaled_sum = local_sum * jnp.exp(local_max - whole_max)
    own_sum, own_pick = (
        lax.psum_scatter(scaled_sum, ("seq", "vocab"), scatter_dimension=0, tiled=True),
        lax.psum_scatter(local_pick, ("seq", "vocab"), scatter_dimension=0, tiled=True),
    )
    own_max = lax.dynamic_slice_in_dim(whole_max, offset, per_device)
    logp = own_pick - own_max - jnp.log(own_sum)
    local_cum = jnp.cumsum(logp)
    device_total = jnp.sum(logp)
    earlier_sum = prefix(device_total, ("seq", "vocab"), add_values, jnp.float32(0.0))
    counts = (offset + jnp.arange(per_device) + 1).astype(jnp.float32)
    own_mean = (earlier_sum + local_cum) / counts
    gathered = lax.all_gather(own_mean[None, :], "logger", axis=0, tiled=True)
    prior = jnp.log(logger_share) - jnp.log(jnp.sum(logger_share))
    shifted = prior[:, None] + gathered
    highest = jnp.max(shifted, axis=0)
    mixture = highest + jnp.log(jnp.sum(jnp.exp(shifted - highest[None, :]), axis=0))
    return (own_mean - mixture)[None, :]


def solution(mesh):
    return jax.shard_map(
        on_device,
        mesh=mesh,
        in_specs=(
            P("logger", ("seq", "vocab"), None),
            P("logger", None, ("seq", "vocab")),
            P(),
            P(),
        ),
        out_specs=P("logger", ("seq", "vocab")),
        check_vma=False,
    )
```

profile of v0, /device:TPU:1, one launch (start us, length us, event | category | flops | bytes accessed | tf_op | source)
XLA Modules:
  0.0 94.9 jit_solution(17818057165997192904)
XLA Ops:
  0.0 0.0 copy-start
  0.0 0.0 copy-start.1
  0.0 0.0 copy-start.2
  0.0 28.0 %all-gather = bf16[1,64,4096]{2,1,0:T(8,128)(2,1)S(1)} all-gather(bf16[1,8,4096]{2,1,0:T(8,128)(2,1)} %param.6), channel_id=2, replica_groups=mesh['logger'=4,'seq'=2,'vocab'=4] {'seq','vocab'}, dimensions={1}, use_global_device_ids=true | all-gather | bytes 589824 | tf_op jit(solution)/shard_map/all_gather | solution.py:38
  28.0 3.1 %fusion.7 = (f32[64]{0:T(128)S(1)}, f32[64,512]{1,0:T(8,128)S(1)}) fusion(bf16[1,4096,512]{2,1,0:T(8,128)(2,1)} %param.7, bf16[1,64,4096]{2,1,0:T(8,128)(2,1)S(1)} %all-gather), kind=kOutput, calls=%fused_computation.17 | convolution fusion | flops 268468160 | bytes 4849920 | tf_op jit(solution)/shard_map/dot_general | solution.py:37
  31.1 0.0 copy-done.1
  31.1 0.2 select_reduce_fusion
  31.3 17.5 %pmax.7 = f32[64]{0:T(128)S(1)} all-reduce(f32[64]{0:T(128)S(1)} %get-tuple-element.45), channel_id=1, replica_groups=mesh['logger'=4,'seq'=2,'vocab'=4] {'seq','vocab'}, use_global_device_ids=true, to_apply=%region_3.4 | all-reduce | flops 64 | bytes 512 | tf_op jit(solution)/shard_map/pmax | solution.py:52
  48.9 13.7 %all-reduce.3 = (f32[64]{0:T(128)S(1)}, f32[64]{0:T(128)S(1)}) all-reduce(f32[64]{0:T(128)S(1)} %exponential_multiply_fusion, f32[64]{0:T(128)S(1)} %get-tuple-element.29), channel_id=4, replica_groups=mesh['logger'=4,'seq'=2,'vocab'=4] {'seq','vocab'}, use_global_device_ids=true, to_apply=%region_5.6.clone | all-reduce | flops 128 | bytes 1024
  62.6 0.0 copy-done
  62.6 0.7 fusion.6
  64.0 0.7 fusion.4
  64.7 0.2 reduce-window.4
  64.9 1.4 %dynamic-update-slice = f32[8]{0:T(128)S(1)} dynamic-update-slice(f32[8]{0:T(128)S(1)} %broadcast.48, f32[1]{0:T(128)} %bitcast.3, u32[]{:T(128)} %bitcast.4) | dynamic-update-slice | bytes 12
  66.3 16.3 %all-reduce = f32[8]{0:T(128)S(1)} all-reduce(f32[8]{0:T(128)S(1)} %dynamic-update-slice), channel_id=1, replica_groups=mesh['logger'=4,'seq'=2,'vocab'=4] {'seq','vocab'}, use_global_device_ids=true, to_apply=%add | all-reduce | flops 8 | bytes 64
  82.6 5.1 %while.10 = (s32[]{:T(128)}, f32[]{:T(128)}, s32[]{:T(128)}, f32[8]{0:T(128)S(1)}, s32[]{:T(128)}, /*index=5*/s32[]{:T(128)}, s32[]{:T(128)}) while((s32[]{:T(128)}, f32[]{:T(128)}, s32[]{:T(128)}, f32[8]{0:T(128)S(1)}, s32[]{:T(128)}, /*index=5*/s32[]{:T(128)}, s32[]{:T(128)}) %tuple.22), condition=%wide.region_8.9_spmd, body=%wide.region_7.8_spmd.sunk | while | flops 6 | bytes 143 | solution.py:15
  82.6 0.6 dynamic_slice.11
  83.9 0.6 dynamic_slice.11
  85.2 0.6 dynamic_slice.11
  86.4 0.6 dynamic_slice.11
  87.7 5.2 %all-gather.1 = f32[4,1,8]{2,1,0:T(1,128)S(1)} all-gather(f32[1,1,8]{2,1,0:T(1,128)S(1)} %fusion.8), channel_id=1, replica_groups=mesh['logger'=4,'seq'=2,'vocab'=4] {'logger'}, dimensions={0}, use_global_device_ids=true | all-gather | bytes 160 | tf_op jit(solution)/shard_map/all_gather | solution.py:65
  92.9 0.0 copy-done.2
  92.9 0.6 reduce_sum.48
  94.2 0.1 add_reduce_fusion
  94.3 0.1 exponential_reduce_fusion.1
  94.4 0.5 bitcast_subtract_fusion
  (5 shorter events, 0.0 us)
Async XLA Ops:
  0.0 62.6 %copy-start = (u32[32]{0:T(128)S(1)}, u32[32]{0:T(128)}, u32[]{:S(2)}) copy-start(u32[32]{0:T(128)} %constant.40) | copy-start | bytes 388
  0.0 31.1 %copy-start.1 = (s32[64]{0:T(128)S(1)}, s32[64]{0:T(128)}, u32[]{:S(2)}) copy-start(s32[64]{0:T(128)} %param.8) | copy-start | bytes 772
  0.0 92.9 %copy-start.2 = (f32[4]{0:T(128)S(1)}, f32[4]{0:T(128)}, u32[]{:S(2)}) copy-start(f32[4]{0:T(128)} %param.9) | copy-start | bytes 52
where the time goes:
time: 95.2 us; the launch traced here: 94.9 us
  blocking collectives  80.7 us (85%)
  local copies, waits for them, and re-layouts  4.51 us (5%)
  matrix products  3.13 us (3%)
  loops' own time  2.63 us (3%)
  other arithmetic  2.46 us (3%)
  between operations  1.46 us (2%)
    unnamed x2, blocking collectives  30 us
    all_gather x1, blocking collectives, on_device(): lax.all_gather(token_rows, ('seq', 'vocab'), axis=0, tiled=True)  28 us
    pmax x1, blocking collectives, on_device(): whole_max = lax.pmax(local_max, ('seq', 'vocab'))  17.5 us
    all_gather x1, blocking collectives, on_device(): gathered = lax.all_gather(own_mean[None, :], 'logger', axis=0, tiled=True)  5.16 us
    dot_general x1, matrix products, on_device(): jnp.dot(lax.all_gather(token_rows, ('seq', 'vocab'), axis=0, tiled=True),...  3.13 us
    another operation x1, loops' own time, prefix(): return lax.fori_loop(0, place, one, state)  2.63 us
    dynamic_slice x4, local copies, waits for them, and re-layouts, one(): return combine(state, lax.dynamic_index_in_dim(gathered, hop, 0, False))  2.45 us
    unnamed x9, local copies, waits for them, and re-layouts  2.06 us

commit v1 on v0

--- a/solution.py
+++ b/solution.py
@@ -2,6 +2,27 @@
 import jax.numpy as jnp
 from jax import lax
 from jax.sharding import PartitionSpec as P
+
+
+def collect(x, axis, dim):
+    devices, index, span = (lax.axis_size(axis), lax.axis_index(axis), x.shape[dim])
+    right = [(i, (i + 1) % devices) for i in range(devices)]
+    backward = [(i, (i - 1) % devices) for i in range(devices)]
+    out = jnp.zeros((*x.shape[:dim], devices * span, *x.shape[dim + 1 :]), x.dtype)
+    out = lax.dynamic_update_slice_in_dim(out, x, index * span, axis=dim)
+    from_left = from_right = x
+    halfway = devices // 2
+    for step in range(1, halfway + 1):
+        from_left = lax.ppermute(from_left, axis, right)
+        out = lax.dynamic_update_slice_in_dim(
+            out, from_left, (index - step) % devices * span, axis=dim
+        )
+        if step < devices - halfway:
+            from_right = lax.ppermute(from_right, axis, backward)
+            out = lax.dynamic_update_slice_in_dim(
+                out, from_right, (index + step) % devices * span, axis=dim
+            )
+    return out
 
 
 def prefix(part, axis, combine, identity):
@@ -35,9 +56,7 @@
     start_carry = (zeros, zeros, zeros)
     start = jnp.int32(0)
     logits = jnp.dot(
-        lax.all_gather(token_rows, ("seq", "vocab"), axis=0, tiled=True),
-        weight,
-        preferred_element_type=jnp.float32,
+        collect(token_rows, ("seq", "vocab"), 0), weight, preferred_element_type=jnp.float32
     )
     block_max = jnp.max(logits, axis=1)
     block_sum = jnp.sum(jnp.exp(logits - block_max[:, None]), axis=1)

time: 95.2 us -> 89.4 us (0.939)
  blocking collectives: 80.7 us -> 50.1 us
  starting transfers between devices: 0 us -> 12.1 us
  waiting for transfers between devices: 0 us -> 9.96 us
  local copies, waits for them, and re-layouts: 4.51 us -> 6.14 us
    all_gather x1 -> x0, blocking collectives: 28 us -> none  [on_device(): lax.all_gather(token_rows, ('seq', 'vocab'), axis=0, tiled=True)]
    ppermute x0 -> x7, starting transfers between devices: none -> 12.1 us  [the longest x3 9.86 us: collect(): from_right = lax.ppermute(from_right, axis, backward)]
    ppermute x0 -> x7, waiting for transfers between devices: none -> 9.96 us  [the longest x4 9.95 us: collect(): from_left = lax.ppermute(from_left, axis, right)]
    pmax x1, blocking collectives: 17.5 us -> 13.7 us  [on_device(): whole_max = lax.pmax(local_max, ('seq', 'vocab'))]
    all_gather x1, blocking collectives: 5.16 us -> 6.28 us  [on_device(): gathered = lax.all_gather(own_mean[None, :], 'logger', axis=0, tiled=True)]
    unnamed x9 -> x7, local copies, waits for them, and re-layouts: 2.06 us -> 2.73 us
  transfers between devices with their start and end apart: 0 -> 7, of which waited for: 0 -> 3; matrix products, arithmetic and copies ran while one was open for 0% -> 4% of each run, Pallas kernels for 0% -> 0%
where the time goes in v1:
time: 89.4 us; the launch traced here: 88.5 us
  blocking collectives  50.1 us (56%)
  starting transfers between devices  12.1 us (14%)
  waiting for transfers between devices  9.96 us (11%)
  local copies, waits for them, and re-layouts  6.14 us (7%)
  matrix products  3.13 us (4%)
  other arithmetic  3.12 us (3%)
  loops' own time  2.65 us (3%)
  between operations  1.42 us (2%)
    unnamed x2, blocking collectives  30.1 us
    pmax x1, blocking collectives, on_device(): whole_max = lax.pmax(local_max, ('seq', 'vocab'))  13.7 us
    ppermute x4, waiting for transfers between devices, collect(): from_left = lax.ppermute(from_left, axis, right)  9.95 us
    ppermute x3, starting transfers between devices, collect(): from_right = lax.ppermute(from_right, axis, backward)  9.86 us
    all_gather x1, blocking collectives, on_device(): gathered = lax.all_gather(own_mean[None, :], 'logger', axis=0, tiled=True)  6.28 us
    dot_general x1, matrix products, on_device(): jnp.dot(collect(token_rows, ('seq', 'vocab'), 0), weight, preferred_eleme...  3.13 us
    unnamed x7, local copies, waits for them, and re-layouts  2.73 us
    another operation x1, loops' own time, prefix(): return lax.fori_loop(0, place, one, state)  2.65 us
  transfers between devices with their start and end apart: 7, of which 3 were waited for; matrix products, arithmetic and copies ran while one was open for 4% of the time, Pallas kernels for 0%

profile of v1, /device:TPU:1, one launch (start us, length us, event | category | flops | bytes accessed | tf_op | source)
XLA Modules:
  0.0 88.5 jit_solution(16486167974854452452)
XLA Ops:
  0.0 0.0 copy-start.1
  0.0 0.0 copy-start
  0.0 2.1 %collective-permute-start = (bf16[8,4096]{1,0:T(8,128)(2,1)}, bf16[8,4096]{1,0:T(8,128)(2,1)S(1)}, u32[]{:S(2)}, u32[]{:S(2)}) collective-permute-start(bf16[8,4096]{1,0:T(8,128)(2,1)} %bitcast.26), channel_id=1, source_target_pairs={{0,1},{1,2},{2,3},{3,4},{4,5},{5,6},{6,7},{7,0},{8,9},{9,10},{10,1... | collective-permute-start | bytes 196616 | tf_op jit(solution)/shard_map/ppermute | solution.py:16
  2.1 2.7 %collective-permute-start.1 = (bf16[8,4096]{1,0:T(8,128)(2,1)}, bf16[8,4096]{1,0:T(8,128)(2,1)S(1)}, u32[]{:S(2)}, u32[]{:S(2)}) collective-permute-start(bf16[8,4096]{1,0:T(8,128)(2,1)} %bitcast.27), channel_id=1, source_target_pairs={{0,7},{1,0},{2,1},{3,2},{4,3},{5,4},{6,5},{7,6},{8,15},{9,8},{10,9... | collective-permute-start | bytes 196616 | tf_op jit(solution)/shard_map/ppermute | solution.py:21
  4.8 1.3 %reduce_sum.48 = f32[]{:T(128)} reduce(f32[4]{0:T(128)} %param.9, f32[]{:T(128)} %constant.67.clone.1), dimensions={0}, to_apply=%region_10.11 | reduce | flops 3 | bytes 24 | tf_op jit(solution)/shard_map/reduce_sum | solution.py:85
  6.1 0.9 constant_dynamic-update-slice_fusion.7
  7.0 1.4 %fusion.5 = (u32[1]{0:T(128)}, u32[1]{0:T(128)}) fusion(u32[32]{0:T(128)} %constant.89, u32[]{:T(128)S(6)} %add.193, u32[]{:T(128)S(6)} %add.196), kind=kLoop, calls=%fused_computation.23 | loop fusion | bytes 24
  9.0 0.0 collective-permute-done
  9.0 0.1 collective-permute-start.2
  9.1 0.0 collective-permute-done.1
  9.1 3.5 %collective-permute-start.3 = (bf16[8,4096]{1,0:T(8,128)(2,1)S(1)}, bf16[8,4096]{1,0:T(8,128)(2,1)S(1)}, u32[]{:S(2)}, u32[]{:S(2)}) collective-permute-start(bf16[8,4096]{1,0:T(8,128)(2,1)S(1)} %collective-permute-done.1), channel_id=1, source_target_pairs={{0,7},{1,0},{2,1},{3,2},{4,3},{5,4},{6,5},{7,6},{8,15},{9,8},{10,9... | collective-permute-start | bytes 196616 | tf_op jit(solution)/shard_map/ppermute | solution.py:21
  12.6 2.5 %collective-permute-done.2 = bf16[8,4096]{1,0:T(8,128)(2,1)S(1)} collective-permute-done((bf16[8,4096]{1,0:T(8,128)(2,1)S(1)}, bf16[8,4096]{1,0:T(8,128)(2,1)S(1)}, u32[]{:S(2)}, u32[]{:S(2)}) %collective-permute-start.2) | collective-permute-done | bytes 65568 | tf_op jit(solution)/shard_map/ppermute | solution.py:16
  15.1 0.0 collective-permute-start.4
  15.1 0.0 collective-permute-done.3
  15.1 3.7 %collective-permute-start.5 = (bf16[8,4096]{1,0:T(8,128)(2,1)S(1)}, bf16[8,4096]{1,0:T(8,128)(2,1)S(1)}, u32[]{:S(2)}, u32[]{:S(2)}) collective-permute-start(bf16[8,4096]{1,0:T(8,128)(2,1)S(1)} %collective-permute-done.3), channel_id=1, source_target_pairs={{0,7},{1,0},{2,1},{3,2},{4,3},{5,4},{6,5},{7,6},{8,15},{9,8},{10,9... | collective-permute-start | bytes 196616 | tf_op jit(solution)/shard_map/ppermute | solution.py:21
  18.8 2.0 %collective-permute-done.4 = bf16[8,4096]{1,0:T(8,128)(2,1)S(1)} collective-permute-done((bf16[8,4096]{1,0:T(8,128)(2,1)S(1)}, bf16[8,4096]{1,0:T(8,128)(2,1)S(1)}, u32[]{:S(2)}, u32[]{:S(2)}) %collective-permute-start.4) | collective-permute-done | bytes 65568 | tf_op jit(solution)/shard_map/ppermute | solution.py:16
  20.8 0.0 collective-permute-start.6
  20.9 0.0 collective-permute-done.5
  20.9 5.4 %collective-permute-done.6 = bf16[8,4096]{1,0:T(8,128)(2,1)S(1)} collective-permute-done((bf16[8,4096]{1,0:T(8,128)(2,1)S(1)}, bf16[8,4096]{1,0:T(8,128)(2,1)S(1)}, u32[]{:S(2)}, u32[]{:S(2)}) %collective-permute-start.6) | collective-permute-done | bytes 65568 | tf_op jit(solution)/shard_map/ppermute | solution.py:16
  26.3 3.1 %fusion.6 = (f32[64]{0:T(128)S(1)}, f32[64,512]{1,0:T(8,128)S(1)}) fusion(bf16[64,4096]{1,0:T(8,128)(2,1)S(1)} %constant_dynamic-update-slice_fusion, bf16[1,4096,512]{2,1,0:T(8,128)(2,1)} %param.7), kind=kOutput, calls=%fused_computation.24 | convolution fusion | flops 268468160 | bytes 4849920 | tf_op jit(solution)/shard_map/dot_general | solution.py:58
  29.5 13.7 %pmax.7 = f32[64]{0:T(128)S(1)} all-reduce(f32[64]{0:T(128)S(1)} %get-tuple-element.45), channel_id=1, replica_groups=mesh['logger'=4,'seq'=2,'vocab'=4] {'seq','vocab'}, use_global_device_ids=true, to_apply=%region_3.4 | all-reduce | flops 64 | bytes 512 | tf_op jit(solution)/shard_map/pmax | solution.py:71
  43.2 0.0 copy-done
  43.2 0.2 select_reduce_fusion
  43.4 16.4 %all-reduce.3 = (f32[64]{0:T(128)S(1)}, f32[64]{0:T(128)S(1)}) all-reduce(f32[64]{0:T(128)S(1)} %exponential_multiply_fusion, f32[64]{0:T(128)S(1)} %get-tuple-element.29), channel_id=3, replica_groups=mesh['logger'=4,'seq'=2,'vocab'=4] {'seq','vocab'}, use_global_device_ids=true, to_apply=%region_5.6.clone | all-reduce | flops 128 | bytes 1024
  59.8 0.7 fusion.3
  60.5 1.3 %dynamic-update-slice = f32[8]{0:T(128)S(1)} dynamic-update-slice(f32[8]{0:T(128)S(1)} %broadcast.55, f32[1]{0:T(128)} %bitcast.3, u32[]{:T(128)} %bitcast.4) | dynamic-update-slice | bytes 12
  62.5 13.7 %all-reduce = f32[8]{0:T(128)S(1)} all-reduce(f32[8]{0:T(128)S(1)} %dynamic-update-slice), channel_id=1, replica_groups=mesh['logger'=4,'seq'=2,'vocab'=4] {'seq','vocab'}, use_global_device_ids=true, to_apply=%add | all-reduce | flops 8 | bytes 64
  76.2 5.1 %while.10 = (s32[]{:T(128)}, f32[]{:T(128)}, s32[]{:T(128)}, f32[8]{0:T(128)S(1)}, s32[]{:T(128)}, /*index=5*/s32[]{:T(128)}, s32[]{:T(128)}) while((s32[]{:T(128)}, f32[]{:T(128)}, s32[]{:T(128)}, f32[8]{0:T(128)S(1)}, s32[]{:T(128)}, /*index=5*/s32[]{:T(128)}, s32[]{:T(128)}) %tuple.22), condition=%wide.region_8.9_spmd, body=%wide.region_7.8_spmd.sunk | while | flops 6 | bytes 135 | solution.py:36
  76.2 0.6 dynamic_slice.11
  77.5 0.6 dynamic_slice.11
  78.8 0.6 dynamic_slice.11
  80.1 0.6 dynamic_slice.11
  81.4 0.2 reduce-window.4
  81.5 0.0 copy-done.1
  81.6 6.3 %all-gather = f32[4,1,8]{2,1,0:T(1,128)S(1)} all-gather(f32[1,1,8]{2,1,0:T(1,128)S(1)} %fusion.8), channel_id=1, replica_groups=mesh['logger'=4,'seq'=2,'vocab'=4] {'logger'}, dimensions={0}, use_global_device_ids=true | all-gather | bytes 160 | tf_op jit(solution)/shard_map/all_gather | solution.py:84
  87.8 0.1 add_reduce_fusion
  87.9 0.1 exponential_reduce_fusion.1
  88.0 0.5 bitcast_subtract_fusion
  (13 shorter events, 0.1 us)
Async XLA Ops:
  0.0 81.5 %copy-start.1 = (f32[4]{0:T(128)S(1)}, f32[4]{0:T(128)}, u32[]{:S(2)}) copy-start(f32[4]{0:T(128)} %param.9) | copy-start | bytes 52
  0.0 43.2 %copy-start = (s32[64]{0:T(128)S(1)}, s32[64]{0:T(128)}, u32[]{:S(2)}) copy-start(s32[64]{0:T(128)} %param.8) | copy-start | bytes 772
  0.0 9.0 %collective-permute-start = (bf16[8,4096]{1,0:T(8,128)(2,1)}, bf16[8,4096]{1,0:T(8,128)(2,1)S(1)}, u32[]{:S(2)}, u32[]{:S(2)}) collective-permute-start(bf16[8,4096]{1,0:T(8,128)(2,1)} %bitcast.26), channel_id=1, source_target_pairs={{0,1},{1,2},{2,3},{3,4},{4,5},{5,6},{6,7},{7,0},{8,9},{9,10},{10,1... | collective-permute-start | bytes 196616 | tf_op jit(solution)/shard_map/ppermute | solution.py:16
  2.1 6.9 %collective-permute-start.1 = (bf16[8,4096]{1,0:T(8,128)(2,1)}, bf16[8,4096]{1,0:T(8,128)(2,1)S(1)}, u32[]{:S(2)}, u32[]{:S(2)}) collective-permute-start(bf16[8,4096]{1,0:T(8,128)(2,1)} %bitcast.27), channel_id=1, source_target_pairs={{0,7},{1,0},{2,1},{3,2},{4,3},{5,4},{6,5},{7,6},{8,15},{9,8},{10,9... | collective-permute-start | bytes 196616 | tf_op jit(solution)/shard_map/ppermute | solution.py:21
  9.0 6.1 %collective-permute-start.2 = (bf16[8,4096]{1,0:T(8,128)(2,1)S(1)}, bf16[8,4096]{1,0:T(8,128)(2,1)S(1)}, u32[]{:S(2)}, u32[]{:S(2)}) collective-permute-start(bf16[8,4096]{1,0:T(8,128)(2,1)S(1)} %collective-permute-done), channel_id=1, source_target_pairs={{0,1},{1,2},{2,3},{3,4},{4,5},{5,6},{6,7},{7,0},{8,9},{9,10},{10,1... | collective-permute-start | bytes 196616 | tf_op jit(solution)/shard_map/ppermute | solution.py:16
  9.1 6.0 %collective-permute-start.3 = (bf16[8,4096]{1,0:T(8,128)(2,1)S(1)}, bf16[8,4096]{1,0:T(8,128)(2,1)S(1)}, u32[]{:S(2)}, u32[]{:S(2)}) collective-permute-start(bf16[8,4096]{1,0:T(8,128)(2,1)S(1)} %collective-permute-done.1), channel_id=1, source_target_pairs={{0,7},{1,0},{2,1},{3,2},{4,3},{5,4},{6,5},{7,6},{8,15},{9,8},{10,9... | collective-permute-start | bytes 196616 | tf_op jit(solution)/shard_map/ppermute | solution.py:21
  15.1 5.8 %collective-permute-start.4 = (bf16[8,4096]{1,0:T(8,128)(2,1)S(1)}, bf16[8,4096]{1,0:T(8,128)(2,1)S(1)}, u32[]{:S(2)}, u32[]{:S(2)}) collective-permute-start(bf16[8,4096]{1,0:T(8,128)(2,1)S(1)} %collective-permute-done.2), channel_id=1, source_target_pairs={{0,1},{1,2},{2,3},{3,4},{4,5},{5,6},{6,7},{7,0},{8,9},{9,10},{10,1... | collective-permute-start | bytes 196616 | tf_op jit(solution)/shard_map/ppermute | solution.py:16
  15.1 5.8 %collective-permute-start.5 = (bf16[8,4096]{1,0:T(8,128)(2,1)S(1)}, bf16[8,4096]{1,0:T(8,128)(2,1)S(1)}, u32[]{:S(2)}, u32[]{:S(2)}) collective-permute-start(bf16[8,4096]{1,0:T(8,128)(2,1)S(1)} %collective-permute-done.3), channel_id=1, source_target_pairs={{0,7},{1,0},{2,1},{3,2},{4,3},{5,4},{6,5},{7,6},{8,15},{9,8},{10,9... | collective-permute-start | bytes 196616 | tf_op jit(solution)/shard_map/ppermute | solution.py:21
  20.8 5.5 %collective-permute-start.6 = (bf16[8,4096]{1,0:T(8,128)(2,1)S(1)}, bf16[8,4096]{1,0:T(8,128)(2,1)S(1)}, u32[]{:S(2)}, u32[]{:S(2)}) collective-permute-start(bf16[8,4096]{1,0:T(8,128)(2,1)S(1)} %collective-permute-done.4), channel_id=1, source_target_pairs={{0,1},{1,2},{2,3},{3,4},{4,5},{5,6},{6,7},{7,0},{8,9},{9,10},{10,1... | collective-permute-start | bytes 196616 | tf_op jit(solution)/shard_map/ppermute | solution.py:16
